TPU v7x, 32 devices: a whole 2x2x4 slice. The times are simulated.
32 devices in a mesh: samp: 4 (over x, core), blk: 8 (over z, y).
Axes of the slice: x: 2, y: 2, z: 4, core: 2. Of those that a mesh axis runs over, the one named last changes fastest.
Arguments:
- inputs: bfloat16 [4, 1024, 1024], P('samp', 'blk'), may hold values from -6 to 6
- cot_first: bfloat16 [4, 1024, 1024], P('samp', 'blk'), may hold values from -6 to 6
- cot_second: bfloat16 [4, 1024, 1024], P('samp', 'blk'), may hold values from -6 to 6
- valid_flags: int32 [4, 1024], P('samp', 'blk'), may hold values from 0 to 1, as said below
- lead_steps: int32 [2, 4], P(None, 'samp'), may hold values from 0 to 7
- masters: float32 [192, 256, 256], P('blk'), may hold values from -4 to 4
- assignment: int32 [192], replicated, may hold values from 0 to 191, as said below
- left_start: float32 [192, 256], P('blk'), may hold values from 256 to 1024
- right_start: float32 [192, 256], P('blk'), may hold values from 256 to 1024
- vectors: float32 [20, 1024], replicated, may hold values from -1.6 to 1.6
- vec_moment: float32 [20, 1024], replicated, may hold values from 0.5 to 8
Outputs:
- pred_first: bfloat16 [4, 1024, 1024], P('samp', 'blk')
- pred_second: bfloat16 [4, 1024, 1024], P('samp', 'blk')
- input_grad: float32 [4, 1024, 1024], P('samp', 'blk')
- matrix_grads: float32 [192, 256, 256], P('blk')
- left_stats: float32 [192, 256, 256], P('blk')
- right_stats: float32 [192, 256, 256], P('blk')
- new_masters: float32 [192, 256, 256], P('blk')
- new_copies: bfloat16 [192, 256, 256], P('blk')
- vec_grads: float32 [20, 1024], replicated
- vec_moments: float32 [20, 1024], replicated
- new_vectors: float32 [20, 1024], replicated
Inputs may be any that keep to these rules, and one draw needn't show every extreme that they name: `valid_flags`: 1 where a patch has data; the first and the last patch of every sample are 1. `assignment`: a permutation of 0 to 191; slots are dealt to the devices of blk in order, 24 each.
All inputs are finite; a program needn't handle non-finite values.
Results may differ from a plain program's by a relative error of at most 0.02.
Values may be sent and summed in bfloat16 or wider, within the bound.
A program may use at most 320 MiB of HBM per device.

v0:
```python
import functools
import math

import jax
import ml_dtypes
import jax.numpy as jnp
from jax import lax
from jax.experimental import pallas as pl
from jax.experimental.pallas import tpu as pltpu
from jax.sharding import PartitionSpec as P

D = 1024
HEADS = 16
FF = 4096
HD = 64
LEADS = 8
BS = 256
ITERS = 6
NB = 192


HIGH = lax.Precision.HIGHEST
step_rate = 0.5
vector_rate = 0.3
masked = 1000000000.0


def assemble(blocks, height, breadth):
    return (
        blocks.reshape(height // BS, breadth // BS, BS, BS)
        .transpose(0, 2, 1, 3)
        .reshape(height, breadth)
    )


def carve(matrix):
    height, breadth = matrix.shape
    return (
        matrix.reshape(height // BS, BS, breadth // BS, BS)
        .transpose(0, 2, 1, 3)
        .reshape(-1, BS, BS)
    )


def unpack(blocks):
    first_end = 3 * D * D // (BS * BS)
    second_end = first_end + D * D // (BS * BS)
    third_end = second_end + D * FF // (BS * BS)
    qkv_weight = assemble(blocks[:first_end], D, 3 * D)
    out_weight = assemble(blocks[first_end:second_end], D, D)
    up_weight = assemble(blocks[second_end:third_end], D, FF)
    down_weight = assemble(blocks[third_end:], FF, D)
    return (qkv_weight, out_weight, up_weight, down_weight)


def norm_layer(value, gain, shift):
    centred = value - jnp.mean(value, axis=-1, keepdims=True)
    spread = jnp.mean(centred * centred, axis=-1, keepdims=True)
    return centred * lax.rsqrt(spread + 1e-06) * gain + shift


def gelu_exact(value):
    return jax.nn.gelu(value, approximate=False)


def heads_of(tensor):
    return tensor.reshape(tensor.shape[0], tensor.shape[1], HEADS, HD)


def split_rows(member, count, width):
    shaped = member.reshape((member.shape[0], count, width) + member.shape[2:])
    return jnp.moveaxis(shaped, 1, 0)


def in_blocks(update, carry, members, length):
    width = math.gcd(length, 1024)
    count = length // width
    if count == 1:
        return update(carry, members, 0)
    stacked = tuple([split_rows(member, count, width) for member in members])
    offsets = jnp.arange(count, dtype=jnp.int32) * width

    def advance(state, item):
        return (update(state, item[0], item[1]), None)

    result, unused = lax.scan(advance, carry, (stacked, offsets))
    return result


def forward_update(query_heads, scaling):

    def update(carry, members, offset):
        running_max, running_sum, weighted = carry
        key_part, value_part, flag_part = members
        bias = (flag_part.astype(jnp.float32) - 1.0) * masked
        scores = (
            jnp.einsum(
                "sqhd,skhd->shqk",
                query_heads,
                heads_of(key_part),
                preferred_element_type=jnp.float32,
            )
            * scaling
            + bias[:, None, None, :]
        )
        new_max = jnp.maximum(running_max, jnp.max(scores, axis=-1))
        shrink = jnp.exp(running_max - new_max)
        expos = jnp.exp(scores - new_max[..., None])
        running_sum = running_sum * shrink + jnp.sum(expos, axis=-1)
        weighted = weighted * shrink[..., None] + jnp.einsum(
            "shqk,skhd->shqd",
            expos.astype(jnp.bfloat16),
            heads_of(value_part),
            preferred_element_type=jnp.float32,
        )
        return (new_max, running_sum, weighted)

    return update


def query_grad_update(query_heads, dout_heads, log_total, inner, scaling):

    def update(carry, members, offset):
        key_part, value_part, flag_part = members
        bias = (flag_part.astype(jnp.float32) - 1.0) * masked
        scores = (
            jnp.einsum(
                "sqhd,skhd->shqk",
                query_heads,
                heads_of(key_part),
                preferred_element_type=jnp.float32,
            )
            * scaling
            + bias[:, None, None, :]
        )
        probs = jnp.exp(scores - log_total[..., None])
        dprobs = jnp.einsum(
            "sqhd,skhd->shqk", dout_heads, heads_of(value_part), preferred_element_type=jnp.float32
        )
        dscores = (probs * (dprobs - inner[..., None])).astype(jnp.bfloat16)
        return (
            carry
            + jnp.einsum(
                "shqk,skhd->sqhd", dscores, heads_of(key_part), preferred_element_type=jnp.float32
            )
            * scaling
        )

    return update


def key_grad_update(key_heads, value_heads, key_bias, total_rows, inner_rows, scaling, anchor):

    def update(carry, members, offset):
        grad_keys, grad_values = carry
        query_part, dout_part = members
        length = query_part.shape[1]
        total_part = jnp.transpose(
            lax.dynamic_slice_in_dim(total_rows, anchor + offset, length, 1), (0, 2, 1)
        )
        inner_part = jnp.transpose(
            lax.dynamic_slice_in_dim(inner_rows, anchor + offset, length, 1), (0, 2, 1)
        )
        query_heads = heads_of(query_part)
        dout_heads = heads_of(dout_part)
        scores = (
            jnp.einsum(
                "sqhd,skhd->shqk", query_heads, key_heads, preferred_element_type=jnp.float32
            )
            * scaling
            + key_bias[:, None, None, :]
        )
        probs = jnp.exp(scores - total_part[..., None])
        dprobs = jnp.einsum(
            "sqhd,skhd->shqk", dout_heads, value_heads, preferred_element_type=jnp.float32
        )
        dscores = (probs * (dprobs - inner_part[..., None])).astype(jnp.bfloat16)
        grad_values = grad_values + jnp.einsum(
            "shqk,sqhd->skhd",
            probs.astype(jnp.bfloat16),
            dout_heads,
            preferred_element_type=jnp.float32,
        )
        grad_keys = (
            grad_keys
            + jnp.einsum(
                "shqk,sqhd->skhd", dscores, query_heads, preferred_element_type=jnp.float32
            )
            * scaling
        )
        return (grad_keys, grad_values)

    return update


def invert_root(stat):
    identity = jnp.eye(stat.shape[0], dtype=jnp.float32)
    frobenius = jnp.sqrt(jnp.sum(stat * stat))
    approx = identity * lax.rsqrt(jnp.sqrt(frobenius))
    moving = stat / frobenius
    for iteration in range(ITERS):
        factor = (5.0 * identity - moving) * 0.25
        approx = jnp.dot(approx, factor, precision=HIGH)
        square = jnp.dot(factor, factor, precision=HIGH)
        moving = jnp.dot(jnp.dot(square, square, precision=HIGH), moving, precision=HIGH)
    return approx


def precondition(gradient, left_diag, right_diag, weight):
    scaled = gradient * lax.rsqrt(jnp.mean(gradient * gradient) + 1e-06)
    identity = jnp.eye(BS, dtype=jnp.float32)
    left_new = 0.5 * identity * left_diag[None, :] + 0.5 * jnp.dot(scaled, scaled.T, precision=HIGH)
    right_new = 0.5 * identity * right_diag[None, :] + 0.5 * jnp.dot(
        scaled.T, scaled, precision=HIGH
    )
    direction = jnp.dot(
        jnp.dot(invert_root(left_new), scaled, precision=HIGH),
        invert_root(right_new),
        precision=HIGH,
    )
    ratio = jnp.sqrt(jnp.mean(weight * weight)) * lax.rsqrt(jnp.mean(direction * direction) + 1e-06)
    return (left_new, right_new, weight - step_rate * ratio * direction)


MESH = pl.DeviceIdType.MESH
LOW = jnp.bfloat16
FULL = jnp.float32
VMEM_ASK = 60 * 1024 * 1024
GROUP = 24
HALF = 12
QUART = 4


def place():
    samp = lax.axis_index("samp")
    blk = lax.axis_index("blk")
    return (lax.div(samp, 2), lax.rem(samp, 2), lax.div(blk, 2), lax.rem(blk, 2))


def meet(devices):
    barrier = pltpu.get_barrier_semaphore()
    for device in devices:
        pl.semaphore_signal(barrier, inc=1, device_id=device, device_id_type=MESH)
    pl.semaphore_wait(barrier, len(devices))


def meet_all():
    barrier = pltpu.get_barrier_semaphore()
    samp = lax.axis_index("samp")
    blk = lax.axis_index("blk")

    def tell(at, carry):
        to = lax.rem(samp * 8 + blk + at, 32)
        pl.semaphore_signal(
            barrier, inc=1, device_id=(lax.div(to, 8), lax.rem(to, 8)), device_id_type=MESH
        )
        return carry

    lax.fori_loop(1, 32, tell, 0)
    pl.semaphore_wait(barrier, 31)


def turned_pair(n):
    return 2 * lax.rem(n, 2) + lax.div(n, 2)


class Swap:
    def __init__(self, local_sems, send_sems, recv_sems, first=0):
        x, c, z, y = place()
        self.first = first
        self.stays = z == turned_pair(2 * x + c)
        self.to = (turned_pair(z), 2 * turned_pair(2 * x + c) + y)
        self.sems = (local_sems, send_sems, recv_sems)
        self.pairs = []

    def start(self, src, dst):
        at = self.first + len(self.pairs)
        local_sems, send_sems, recv_sems = self.sems
        local = pltpu.make_async_copy(src, dst, local_sems.at[at])
        away = pltpu.make_async_remote_copy(
            src_ref=src, dst_ref=dst, send_sem=send_sems.at[at], recv_sem=recv_sems.at[at],
            device_id=self.to, device_id_type=MESH,
        )
        self.pairs.append((local, away))

        @pl.when(self.stays)
        def keep():
            local.start()

        @pl.when(jnp.logical_not(self.stays))
        def send():
            away.start()

    def finish(self):
        @pl.when(self.stays)
        def kept():
            for local, away in self.pairs:
                local.wait()

        @pl.when(jnp.logical_not(self.stays))
        def sent():
            for local, away in self.pairs:
                away.wait()


def push(src, dst, send, recv, device):
    copy = pltpu.make_async_remote_copy(
        src_ref=src, dst_ref=dst, send_sem=send, recv_sem=recv, device_id=device, device_id_type=MESH
    )
    copy.start()
    return copy


FIRST, SECOND, BOTH, CROSS = range(4)
SIZES = (2, 2, 3, 1)


def gather_blocks(r, notes, while_last):
    x, c, z, y = place()
    samp = 2 * x + c
    blk = 2 * z + y
    to_y = (samp, 2 * z + 1 - y)
    to_x = (2 * (1 - x) + c, blk)
    to_c = (2 * x + 1 - c, blk)
    base = c * HALF
    out = r.weights
    starts = (base + x * 8, base + x * 8 + 2, base + QUART, base + QUART + 3)
    far_starts = (base + (1 - x) * 8, base + (1 - x) * 8 + 2)
    other = (1 - c) * HALF
    parts = [base + x * 8, base + QUART, base + (1 - x) * 8, other, other + QUART, other + 2 * QUART]
    notes_out, note_send, note_recv = r.notes_land, r.note_send, r.note_recv

    def load(at):
        return pltpu.make_async_copy(
            r.masters.at[pl.ds(parts[at], QUART)], r.wide.at[at % 2], r.load_sems.at[at]
        )

    def ready(at):
        load(at).wait()
        out[pl.ds(blk * GROUP + parts[at], QUART)] = r.wide[at % 2].astype(LOW)
        if at + 2 < len(parts):
            load(at + 2).start()

    def copy(group, start, size, sems, at, device):
        place_out = out.at[pl.ds(group * GROUP + start, size)]
        return pltpu.make_async_remote_copy(
            src_ref=place_out, dst_ref=place_out,
            send_sem=sems.at[(0,) + at], recv_sem=sems.at[(1,) + at], device_id=device, device_id_type=MESH,
        )

    def z_copy(kind, way, origin):
        to = (samp, blk + (2 if way == 0 else -2))
        return copy(2 * origin + y, starts[kind], SIZES[kind], r.z_sems, (kind, way, origin), to)

    def z_cross(way, origin, side):
        to = (samp, blk + (2 if way == 0 else -2))
        return copy(2 * origin + side, starts[CROSS], 1, r.z_sems, (CROSS + side, way, origin), to)

    def y_copy(kind, origin):
        return copy(2 * origin + y, starts[kind], SIZES[kind], r.y_sems, (kind, origin), to_y)

    def y_landed(kind, origin):
        return copy(2 * origin + 1 - y, starts[kind], SIZES[kind], r.y_sems, (kind, origin), to_y)

    def x_copy(kind, group):
        return copy(group, starts[kind], SIZES[kind], r.x_sems, (kind, group), to_x)

    def x_landed(kind, group):
        return copy(group, far_starts[kind], SIZES[kind], r.x_sems, (kind, group), to_x)

    def core_copy(kind, group):
        return copy(group, starts[kind], SIZES[kind], r.core_sems, (kind, group), to_c)

    def far_copy(kind, group):
        return copy(group, far_starts[kind], SIZES[kind], r.far_sems, (kind, group), to_c)

    def on_from_here(kind, group):
        if kind in (FIRST, SECOND):
            x_copy(kind, group).start()
        core_copy(kind, group).start()

    def begin(kind):
        @pl.when(z < 3)
        def up():
            z_copy(kind, 0, z).start()

        @pl.when(z > 0)
        def down():
            z_copy(kind, 1, z).start()

        y_copy(kind, z).start()

    def z_step(kind, distance):
        for way in (0, 1):
            origin = z - distance if way == 0 else z + distance

            @pl.when(origin >= 0 if way == 0 else origin <= 3)
            def arrived():
                z_copy(kind, way, origin).wait_recv()

                @pl.when(z < 3 if way == 0 else z > 0)
                def onward():
                    z_copy(kind, way, origin).start()

                y_copy(kind, origin).start()
                on_from_here(kind, 2 * origin + y)

    def y_step(kind, distance):
        for way in (0, 1):
            origin = z - distance if way == 0 else z + distance

            @pl.when(origin >= 0 if way == 0 else origin <= 3)
            def arrived():
                y_landed(kind, origin).wait_recv()
                on_from_here(kind, 2 * origin + 1 - y)

    def y_own(kind):
        y_landed(kind, z).wait_recv()
        on_from_here(kind, 2 * z + 1 - y)

    def cross_step(distance):
        for side in (0, 1):
            for way in (0, 1):
                origin = z - distance if way == 0 else z + distance

                @pl.when(origin >= 0 if way == 0 else origin <= 3)
                def arrived():
                    z_cross(way, origin, side).wait_recv()

                    @pl.when(z < 3 if way == 0 else z > 0)
                    def onward():
                        z_cross(way, origin, side).start()

                    core_copy(CROSS, 2 * origin + side).start()

    def x_step(kind, distance, same):
        for way in (0, 1):
            origin = z - distance if way == 0 else z + distance

            @pl.when(origin >= 0 if way == 0 else origin <= 3)
            def arrived():
                group = 2 * origin + (y if same else 1 - y)
                x_landed(kind, group).wait_recv()
                far_copy(kind, group).start()

    def x_own(kind):
        x_landed(kind, 2 * z + 1 - y).wait_recv()
        far_copy(kind, 2 * z + 1 - y).start()

    note_local = pltpu.make_async_copy(notes, notes_out.at[blk], r.load_sems.at[6])

    def note_copy(j, origin):
        return pltpu.make_async_remote_copy(
            src_ref=notes, dst_ref=notes_out.at[origin], send_sem=note_send.at[j], recv_sem=note_recv.at[origin],
            device_id=(j // 2, 2 * turned_pair(samp) + j % 2), device_id_type=MESH,
        )

    stays = z == turned_pair(samp)

    def is_me(j):
        return jnp.logical_and(stays, 2 * samp + y == j)

    def here_from(j):
        return jnp.logical_and(stays, blk == j)

    load(0).start()
    load(1).start()
    meet_all()
    r.swap_rows.start(r.rows_in, r.rows_land)
    def cross_begin():
        y_landed(CROSS, z).wait_recv()
        core_copy(CROSS, 2 * z + 1 - y).start()
        for way, there in ((0, z < 3), (1, z > 0)):
            for side in (0, 1):
                @pl.when(there)
                def both_sides():
                    z_cross(way, z, side).start()

    ready(0)
    begin(FIRST)
    begin(SECOND)
    ready(1)
    y_copy(CROSS, z).start()
    for j in range(8):

        @pl.when(jnp.logical_not(is_me(j)))
        def send_note():
            note_copy(j, blk).start()

    @pl.when(stays)
    def keep_note():
        note_local.start()

    for at in range(2, len(parts)):
        ready(at)
    z_step(FIRST, 1)
    z_step(SECOND, 1)
    y_own(SECOND)
    z_step(FIRST, 2)
    begin(BOTH)
    z_step(SECOND, 2)
    y_step(FIRST, 1)
    y_own(FIRST)
    y_own(BOTH)
    z_step(SECOND, 3)
    x_step(FIRST, 1, True)
    y_step(SECOND, 1)
    x_own(SECOND)
    z_step(BOTH, 1)
    cross_begin()
    x_step(FIRST, 2, True)
    z_step(FIRST, 3)
    y_step(FIRST, 2)
    cross_step(1)
    x_step(SECOND, 1, True)
    x_own(FIRST)
    y_step(SECOND, 2)
    y_step(SECOND, 3)
    x_step(FIRST, 1, False)
    z_step(BOTH, 2)
    x_step(SECOND, 1, False)
    y_step(BOTH, 1)
    x_step(FIRST, 2, False)
    z_step(BOTH, 3)
    x_step(SECOND, 2, True)
    y_step(FIRST, 3)
    x_step(FIRST, 3, True)
    cross_step(2)
    y_step(BOTH, 2)
    x_step(SECOND, 3, False)
    x_step(SECOND, 2, False)
    x_step(SECOND, 3, True)
    cross_step(3)
    y_step(BOTH, 3)
    x_step(FIRST, 3, False)

    while_last()
    other_starts = (other + x * 8, other + x * 8 + 2, other + QUART, other + QUART + 3)
    other_far = (other + (1 - x) * 8, other + (1 - x) * 8 + 2)

    def settle(group, carry):
        @pl.when(group != blk)
        def other_group():
            for kind in range(4):
                copy(group, other_starts[kind], SIZES[kind], r.core_sems, (kind, group), to_c).wait_recv()
                core_copy(kind, group).wait_send()
            for kind in (FIRST, SECOND):
                copy(group, other_far[kind], SIZES[kind], r.far_sems, (kind, group), to_c).wait_recv()
                far_copy(kind, group).wait_send()
                x_copy(kind, group).wait_send()

        return carry

    lax.fori_loop(0, 8, settle, 0)

    def sent_along(origin, carry):
        for kind in (FIRST, SECOND, BOTH):
            y_copy(kind, origin).wait_send()

            @pl.when(jnp.logical_and(origin <= z, z < 3))
            def up():
                z_copy(kind, 0, origin).wait_send()

            @pl.when(jnp.logical_and(origin >= z, z > 0))
            def down():
                z_copy(kind, 1, origin).wait_send()

        for side in (0, 1):
            @pl.when(jnp.logical_and(origin <= z, z < 3))
            def cross_up():
                z_cross(0, origin, side).wait_send()

            @pl.when(jnp.logical_and(origin >= z, z > 0))
            def cross_down():
                z_cross(1, origin, side).wait_send()

        return carry

    lax.fori_loop(0, 4, sent_along, 0)
    y_copy(CROSS, z).wait_send()
    for j in range(8):

        @pl.when(jnp.logical_not(is_me(j)))
        def sent_note():
            note_copy(j, blk).wait_send()

        @pl.when(jnp.logical_not(here_from(j)))
        def got_note():
            note_copy(j, j).wait_recv()

    @pl.when(stays)
    def kept_note():
        note_local.wait()


def local_any(
    inputs,
    cot_first,
    cot_second,
    valid_flags,
    lead_steps,
    masters,
    assignment,
    left_start,
    right_start,
    vectors,
    vec_moment,
):
    copies = lax.all_gather(masters.astype(jnp.bfloat16), "blk", axis=0, tiled=True)
    blocks = jnp.take(copies, assignment, axis=0)
    qkv_weight, out_weight, up_weight, down_weight = unpack(blocks)
    scaling = HD ** (-0.5)
    flags_low = valid_flags.astype(jnp.bfloat16)
    key_bias = (valid_flags.astype(jnp.float32) - 1.0) * masked
    lead_base = 8 + FF // D
    lead_table = vectors[lead_base:]
    samples = inputs.shape[0]
    patches = inputs.shape[1]

    def forward(hidden_in, lead_ids):
        chosen = (lead_ids[:, None] == jnp.arange(LEADS, dtype=jnp.int32)[None, :]).astype(
            jnp.float32
        )
        lead_rows = jnp.dot(chosen, lead_table, precision=HIGH)
        hidden = hidden_in + lead_rows[:, None, :]
        normed_low = norm_layer(hidden, vectors[0], vectors[1]).astype(jnp.bfloat16)
        packed = jnp.einsum(
            "spd,de->spe", normed_low, qkv_weight, preferred_element_type=jnp.float32
        )
        queries = (packed[..., :D] + vectors[2]).astype(jnp.bfloat16)
        keys_low = packed[..., D : 2 * D].astype(jnp.bfloat16)
        values_low = (packed[..., 2 * D :] + vectors[3]).astype(jnp.bfloat16)
        start_state = (
            jnp.full((samples, HEADS, patches), -1e30, jnp.float32),
            jnp.zeros((samples, HEADS, patches), jnp.float32),
            jnp.zeros((samples, HEADS, patches, HD), jnp.float32),
        )
        update = forward_update(heads_of(queries), scaling)
        gathered = None
        piece = (
            lax.all_gather(keys_low, "blk", axis=1, tiled=True),
            lax.all_gather(values_low, "blk", axis=1, tiled=True),
            lax.all_gather(flags_low, "blk", axis=1, tiled=True),
        )
        running_max, running_sum, weighted = in_blocks(
            update, start_state, piece, piece[0].shape[1]
        )
        attended = jnp.transpose(weighted / running_sum[..., None], (0, 2, 1, 3)).reshape(
            samples, patches, D
        )
        log_total = running_max + jnp.log(running_sum)
        attended_low = attended.astype(jnp.bfloat16)
        middle = (
            hidden
            + jnp.einsum(
                "spd,de->spe", attended_low, out_weight, preferred_element_type=jnp.float32
            )
            + vectors[4]
        )
        normed_two = norm_layer(middle, vectors[5], vectors[6]).astype(jnp.bfloat16)
        upward = jnp.einsum(
            "spd,df->spf", normed_two, up_weight, preferred_element_type=jnp.float32
        ) + vectors[8:lead_base].reshape(FF)
        activated = gelu_exact(upward).astype(jnp.bfloat16)
        result = (
            middle
            + jnp.einsum("spf,fd->spd", activated, down_weight, preferred_element_type=jnp.float32)
            + vectors[7]
        )
        saved = (
            hidden,
            normed_low,
            queries,
            keys_low,
            values_low,
            attended,
            attended_low,
            log_total,
            middle,
            normed_two,
            upward,
            activated,
            chosen,
            gathered,
        )
        return (result, saved)

    def backward(grad_out, saved):
        (
            hidden,
            normed_low,
            queries,
            keys_low,
            values_low,
            attended,
            attended_low,
            log_total,
            middle,
            normed_two,
            upward,
            activated,
            chosen,
            gathered,
        ) = saved
        grad_two = grad_out.astype(jnp.bfloat16)
        down_grad = jnp.einsum(
            "spf,spd->fd", activated, grad_two, preferred_element_type=jnp.float32
        )
        down_bias = jnp.sum(grad_two.astype(jnp.float32), axis=(0, 1))
        grad_act = jnp.einsum(
            "spd,fd->spf", grad_two, down_weight, preferred_element_type=jnp.float32
        )
        gelu_value, gelu_pull = jax.vjp(gelu_exact, upward)
        grad_up = gelu_pull(grad_act)[0].astype(jnp.bfloat16)
        up_grad = jnp.einsum("spd,spf->df", normed_two, grad_up, preferred_element_type=jnp.float32)
        up_bias = jnp.sum(grad_up.astype(jnp.float32), axis=(0, 1))
        grad_normed_two = jnp.einsum(
            "spf,df->spd", grad_up, up_weight, preferred_element_type=jnp.float32
        )
        norm_value, norm_pull = jax.vjp(norm_layer, middle, vectors[5], vectors[6])
        grad_middle_norm, gain_two, shift_two = norm_pull(grad_normed_two)
        grad_middle = grad_out + grad_middle_norm
        grad_one = grad_middle.astype(jnp.bfloat16)
        out_grad = jnp.einsum(
            "spd,spe->de", attended_low, grad_one, preferred_element_type=jnp.float32
        )
        out_bias = jnp.sum(grad_one.astype(jnp.float32), axis=(0, 1))
        grad_attended = jnp.einsum(
            "spe,de->spd", grad_one, out_weight, preferred_element_type=jnp.float32
        ).astype(jnp.bfloat16)
        inner = jnp.sum(
            (grad_attended.astype(jnp.float32) * attended).reshape(samples, patches, HEADS, HD),
            axis=-1,
        )
        inner_heads = jnp.transpose(inner, (0, 2, 1))
        zero_query = jnp.zeros((samples, patches, HEADS, HD), jnp.float32)
        update_query = query_grad_update(
            heads_of(queries), heads_of(grad_attended), log_total, inner_heads, scaling
        )
        piece = (
            lax.all_gather(keys_low, "blk", axis=1, tiled=True),
            lax.all_gather(values_low, "blk", axis=1, tiled=True),
            lax.all_gather(flags_low, "blk", axis=1, tiled=True),
        )
        grad_query = in_blocks(update_query, zero_query, piece, piece[0].shape[1])
        total_rows, inner_rows = (
            lax.all_gather(jnp.transpose(log_total, (0, 2, 1)), "blk", axis=1, tiled=True),
            lax.all_gather(inner, "blk", axis=1, tiled=True),
        )
        key_heads = heads_of(keys_low)
        value_heads = heads_of(values_low)
        zero_pair = (zero_query, zero_query)
        piece = (
            lax.all_gather(queries, "blk", axis=1, tiled=True),
            lax.all_gather(grad_attended, "blk", axis=1, tiled=True),
        )
        update_keys = key_grad_update(
            key_heads, value_heads, key_bias, total_rows, inner_rows, scaling, jnp.int32(0)
        )
        grad_keys, grad_values = in_blocks(update_keys, zero_pair, piece, piece[0].shape[1])
        grad_packed = jnp.concatenate(
            [
                grad_query.reshape(samples, patches, D),
                grad_keys.reshape(samples, patches, D),
                grad_values.reshape(samples, patches, D),
            ],
            axis=-1,
        ).astype(jnp.bfloat16)
        qkv_grad = jnp.einsum(
            "spd,spe->de", normed_low, grad_packed, preferred_element_type=jnp.float32
        )
        query_bias = jnp.sum(grad_packed[..., :D].astype(jnp.float32), axis=(0, 1))
        value_bias = jnp.sum(grad_packed[..., 2 * D :].astype(jnp.float32), axis=(0, 1))
        grad_normed = jnp.einsum(
            "spe,de->spd", grad_packed, qkv_weight, preferred_element_type=jnp.float32
        )
        first_value, first_pull = jax.vjp(norm_layer, hidden, vectors[0], vectors[1])
        grad_hidden_norm, gain_one, shift_one = first_pull(grad_normed)
        grad_hidden = grad_middle + grad_hidden_norm
        lead_grad = jnp.dot(chosen.T, jnp.sum(grad_hidden, axis=1), precision=HIGH)
        vec_rows = jnp.concatenate(
            [
                gain_one[None],
                shift_one[None],
                query_bias[None],
                value_bias[None],
                out_bias[None],
                gain_two[None],
                shift_two[None],
                down_bias[None],
                up_bias.reshape(FF // D, D),
                lead_grad,
            ],
            axis=0,
        )
        return (grad_hidden, (qkv_grad, out_grad, up_grad, down_grad), vec_rows)

    earlier, saved_one = forward(inputs.astype(jnp.float32), lead_steps[0])
    later, saved_two = forward(earlier, lead_steps[1])
    grad_between, mats_two, vec_two = backward(cot_second.astype(jnp.float32), saved_two)
    input_grad, mats_one, vec_one = backward(
        cot_first.astype(jnp.float32) + grad_between, saved_one
    )
    grad_blocks = jnp.concatenate(
        [
            carve(mats_one[0] + mats_two[0]),
            carve(mats_one[1] + mats_two[1]),
            carve(mats_one[2] + mats_two[2]),
            carve(mats_one[3] + mats_two[3]),
        ],
        axis=0,
    )
    position = jnp.arange(NB, dtype=jnp.int32)
    inverse = jnp.sum(
        jnp.where(assignment[None, :] == position[:, None], position[None, :], 0), axis=1
    )
    slotted = jnp.take(grad_blocks, inverse, axis=0)
    shared = lax.psum_scatter(slotted, "blk", scatter_dimension=0, tiled=True)
    matrix_grads = lax.psum(shared.astype(jnp.bfloat16), "samp").astype(jnp.float32)
    vec_grads = lax.psum(vec_one + vec_two, ("samp", "blk"))
    left_stats, right_stats, new_masters = jax.vmap(precondition)(
        matrix_grads, left_start, right_start, masters
    )
    scaled_vec = vec_grads * lax.rsqrt(
        jnp.mean(vec_grads * vec_grads, axis=1, keepdims=True) + 1e-06
    )
    vec_moments = 0.5 * vec_moment + 0.5 * scaled_vec * scaled_vec
    new_vectors = vectors - vector_rate * scaled_vec * lax.rsqrt(vec_moments)
    return (
        earlier.astype(jnp.bfloat16),
        later.astype(jnp.bfloat16),
        input_grad,
        matrix_grads,
        left_stats,
        right_stats,
        new_masters,
        new_masters.astype(jnp.bfloat16),
        vec_grads,
        vec_moments,
        new_vectors,
    )


TOKENS = 128
PAIR = 2 * HD
SEQ_ALL = 8 * TOKENS
QKV_AT, OUT_AT, UP_AT, DOWN_AT = 0, 48, 64, 128
WIDE = D // BS
DEEP = FF // BS
LEAD_AT = 8 + FF // D


def dot(left, right):
    return jnp.dot(left, right, preferred_element_type=FULL)


def dot_t(left, right):
    return lax.dot_general(left, right, (((1,), (1,)), ((), ())), preferred_element_type=FULL)


def normal(value):
    centred = value - jnp.mean(value, axis=-1, keepdims=True)
    rate = lax.rsqrt(jnp.mean(centred * centred, axis=-1, keepdims=True) + 1e-06)
    return (centred * rate, rate)


def normal_back(grad, unit, rate, gain):
    scaled = grad * gain
    return rate * (
        scaled
        - jnp.mean(scaled, axis=-1, keepdims=True)
        - unit * jnp.mean(scaled * unit, axis=-1, keepdims=True)
    )


def total(value):
    return jnp.sum(value, axis=0, keepdims=True)


def gelu_parts(value):
    phi = 0.5 + 0.5 * lax.erf(value * (0.5**0.5))
    return phi, value * phi


def gelu_slope(value, phi):
    return phi + value * jnp.exp(-0.5 * value * value) * ((2.0 * math.pi) ** -0.5)


class Weights:
    def __init__(self, slots, held):
        self.slots, self.held = slots, held

    def block(self, base, cols, row, col):
        return self.held[self.slots[base + row * cols + col]]

    def down_col(self, base, rows, cols, col):
        return jnp.concatenate([self.block(base, cols, row, col) for row in range(rows)], axis=0)

    def along_row(self, base, cols, row, first=0, last=None):
        return jnp.concatenate(
            [self.block(base, cols, row, col) for col in range(first, cols if last is None else last)], axis=1
        )


def lead_row(vecs, lead):
    row = jnp.zeros((1, D), FULL)
    for at in range(LEADS):
        row = row + jnp.where(lead == at, vecs[LEAD_AT + at : LEAD_AT + at + 1], 0.0)
    return row


def project(r, layer, hidden, vecs, weights):
    unit, unused = normal(hidden)
    normed = (unit * vecs[0:1] + vecs[1:2]).astype(LOW)
    for k in range(WIDE):
        r.left_held[layer, k] = normed[:, k * BS : (k + 1) * BS].T
    give_pool(r, True, layer, 0)
    for kind in (1, 0, 2):
        for step in range(WIDE):
            within = lax.rem(step + lax.div(r.plane.me, 2), WIDE)
            part = dot(normed, weights.down_col(QKV_AT, WIDE, 3 * WIDE, kind * WIDE + within))
            if kind != 1:
                row = 2 if kind == 0 else 3
                part = part + vecs[row : row + 1, pl.ds(pl.multiple_of(within * BS, BS), BS)]
            part = part.astype(LOW)
            for half in range(2):
                r.packed[kind, 2 * within + half] = part[:, half * PAIR : (half + 1) * PAIR]
                r.plane.send_or_keep(
                    r.packed.at[kind], r.held[layer].at[kind], r.in_sems[layer].at[kind], 2 * within + half
                )


def pool_at(left, kind):
    counts, bases = (LEFTS, LEFT_AT) if left else (RIGHTS, RIGHT_AT)
    return pl.ds(bases[kind], counts[kind])


def pool_copies(r, left, layer, kind):
    x, c, z, y = place()
    ids = pool_at(left, kind)
    at = (0 if left else 8) + 4 * layer + kind
    source = (r.left_held if left else r.right_held).at[layer, ids]

    def target(part):
        tokens = pl.ds((2 * part + layer) * TOKENS, TOKENS)
        return r.left_pool.at[ids, :, tokens] if left else r.right_pool.at[ids, tokens]

    here = pltpu.make_async_copy(source, target(0), r.pool_sems.at[0, at])
    there = pltpu.make_async_remote_copy(
        src_ref=source, dst_ref=target(1), send_sem=r.pool_sems.at[1, at], recv_sem=r.pool_sems.at[2, at],
        device_id=(2 * x + 1 - c, 2 * z + y), device_id_type=MESH,
    )
    return here, there


def give_pool(r, left, layer, kind):
    for copy in pool_copies(r, left, layer, kind):
        copy.start()


def feed(r, layer, hidden, vecs, weights, slope_held):
    attended = jnp.concatenate([r.o_land[j] for j in range(8)], axis=1)
    for k in range(WIDE):
        r.left_held[layer, WIDE + k] = attended[:, k * BS : (k + 1) * BS].T
    give_pool(r, True, layer, 1)
    branch = [dot(attended, weights.down_col(OUT_AT, WIDE, WIDE, n)) for n in range(WIDE)]
    middle = hidden + jnp.concatenate(branch, axis=1) + vecs[4:5]
    unit, unused = normal(middle)
    normed = (unit * vecs[5:6] + vecs[6:7]).astype(LOW)
    for k in range(WIDE):
        r.left_held[layer, 2 * WIDE + k] = normed[:, k * BS : (k + 1) * BS].T
    give_pool(r, True, layer, 2)
    per = D // BS
    for f in range(DEEP):
        bias = vecs[8 + f // per : 9 + f // per, (f % per) * BS : (f % per + 1) * BS]
        upward = dot(normed, weights.down_col(UP_AT, WIDE, DEEP, f)) + bias
        phi, activated = gelu_parts(upward)
        slope_held[f] = gelu_slope(upward, phi)
        activated = activated.astype(LOW)
        r.act_held[:, f * BS : (f + 1) * BS] = activated
        r.left_held[layer, 3 * WIDE + f] = activated.T
    give_pool(r, True, layer, 3)
    branch = [dot(r.act_held[...], weights.down_col(DOWN_AT, DEEP, WIDE, n)) for n in range(WIDE)]
    return middle, middle + jnp.concatenate(branch, axis=1) + vecs[7:8]


def feed_back(r, layer, grad_out, middle, slope_in, vecs, weights):
    rows = r.rows
    grad_two = grad_out.astype(LOW)
    for k in range(WIDE):
        r.right_held[layer, RIGHT_AT[3] + k] = grad_two[:, k * BS : (k + 1) * BS]
    give_pool(r, False, layer, 3)
    rows[7:8] += total(grad_two.astype(FULL))
    per = D // BS
    for f in range(DEEP):
        grad_act = dot_t(grad_two, weights.along_row(DOWN_AT, WIDE, f))
        grad_up = (grad_act * slope_in[f]).astype(LOW)
        r.right_held[layer, RIGHT_AT[2] + f] = grad_up
        rows[8 + f // per : 9 + f // per, (f % per) * BS : (f % per + 1) * BS] += total(grad_up.astype(FULL))
    give_pool(r, False, layer, 2)
    grad_up = jnp.concatenate([r.right_held[layer, RIGHT_AT[2] + f] for f in range(DEEP)], axis=1)
    grad_normed = jnp.concatenate(
        [dot_t(grad_up, weights.along_row(UP_AT, DEEP, k)) for k in range(WIDE)], axis=1
    )
    unit, rate = normal(middle)
    rows[5:6] += total(grad_normed * unit)
    rows[6:7] += total(grad_normed)
    grad_middle = grad_out + normal_back(grad_normed, unit, rate, vecs[5:6])
    grad_one = grad_middle.astype(LOW)
    for k in range(WIDE):
        r.right_held[layer, RIGHT_AT[1] + k] = grad_one[:, k * BS : (k + 1) * BS]
    give_pool(r, False, layer, 1)
    rows[4:5] += total(grad_one.astype(FULL))
    for k in range(WIDE):
        part = dot_t(grad_one, weights.along_row(OUT_AT, WIDE, k)).astype(LOW)
        for half in range(2):
            r.do_message[2 * k + half] = part[:, half * PAIR : (half + 1) * PAIR]
            r.plane.send_or_keep(r.do_message, r.do_land, r.do_sems[layer], 2 * k + half)
    return grad_middle


def project_back(r, layer, grad_middle, hidden, vecs, weights, lead):
    rows = r.rows

    def blocks_of_kind(kind):
        source, cols = (r.dq_land, slice(0, PAIR)) if kind == 0 else (r.dkv_land, slice((kind - 1) * PAIR, kind * PAIR))
        for within in range(WIDE):
            part = jnp.concatenate([source[2 * within, :, cols], source[2 * within + 1, :, cols]], axis=1)
            r.right_held[layer, kind * WIDE + within] = part
            if kind != 1:
                row = 2 if kind == 0 else 3
                rows[row : row + 1, within * BS : (within + 1) * BS] += total(part.astype(FULL))

    def back(first, last):
        part = jnp.concatenate([r.right_held[layer, n] for n in range(first, last)], axis=1)
        return jnp.concatenate(
            [dot_t(part, weights.along_row(QKV_AT, 3 * WIDE, k, first, last)) for k in range(WIDE)], axis=1
        )

    r.plane.received(r.dkv_land, r.dkv_sems[layer])
    blocks_of_kind(1)
    blocks_of_kind(2)
    grad_normed = back(WIDE, 3 * WIDE)
    r.plane.received(r.dq_land, r.dq_sems[layer])
    blocks_of_kind(0)
    give_pool(r, False, layer, 0)
    grad_normed = grad_normed + back(0, WIDE)
    unit, rate = normal(hidden)
    rows[0:1] += total(grad_normed * unit)
    rows[1:2] += total(grad_normed)
    grad_hidden = grad_middle + normal_back(grad_normed, unit, rate, vecs[0:1])
    sums = total(grad_hidden)
    for at in range(LEADS):
        rows[LEAD_AT + at : LEAD_AT + at + 1] += jnp.where(lead == at, sums, 0.0)
    return grad_hidden


def attend(r, layer):
    held, turned, stats, sems = r.held[layer], r.turned[layer], r.stats[layer], r.in_sems[layer]
    plane = r.plane
    plane.received(held.at[1], sems.at[1])
    keys = held[1].reshape(SEQ_ALL, PAIR).astype(FULL)
    for head in range(2):
        r.key_side[head] = key_columns(keys, r.neg[...], head).astype(LOW)

    def chunk(step, carry):
        at = lax.rem(step + lax.div(plane.me, 2), 4)
        first = pl.multiple_of(at * BS, BS)
        for half in range(2):
            plane.received_from(held.at[0], sems.at[0], 2 * at + half)
        queries = held[0, pl.ds(2 * at, 2)].reshape(BS, PAIR).astype(FULL)
        scales = []
        for head in range(2):
            scores = dot_t(r.key_side[head], query_columns(queries, head).astype(LOW))
            most = jnp.max(scores, axis=0, keepdims=True)
            expos = jnp.exp(scores - most)
            sums = jnp.sum(expos, axis=0, keepdims=True)
            r.expos[head] = expos.astype(LOW)
            stats[head : head + 1, pl.ds(first, BS)] = most + jnp.log(sums)
            scales.append(1.0 / sums)

        @pl.when(step == 0)
        def values_in():
            plane.received(held.at[2], sems.at[2])
            r.values_t[...] = held[2].reshape(SEQ_ALL, PAIR).T

        for head in range(2):
            side = slice(head * HD, (head + 1) * HD)
            turned[at, side] = dot(r.values_t[side], r.expos[head]) * scales[head]
        for half in range(2):
            to = 2 * at + half
            r.o_message[to] = turned[at, :, half * TOKENS : (half + 1) * TOKENS].astype(LOW).T
            plane.send_or_keep(r.o_message, r.o_land, r.o_sems[layer], to)
        return carry

    lax.fori_loop(0, SEQ_ALL // BS, chunk, 0)
    for kind in range(3):
        plane.sent(r.packed.at[kind], sems.at[kind])
    plane.received(r.o_land, r.o_sems[layer])
    plane.sent(r.o_message, r.o_sems[layer])


def attend_back(r, layer):
    held, turned, stats = r.held[layer], r.turned[layer], r.stats[layer]
    plane = r.plane
    queries = held[0].reshape(SEQ_ALL, PAIR).astype(FULL)
    keys = held[1].reshape(SEQ_ALL, PAIR).astype(FULL)
    keys_t = held[1].reshape(SEQ_ALL, PAIR).T
    r.grad_q[...] = jnp.zeros_like(r.grad_q)
    for head in range(2):
        side = query_columns(queries, head)
        r.query_side[head] = side.astype(LOW)
        r.query_plain[head] = jnp.where(own_columns(queries, head)[0], side, 0.0).astype(LOW)
        r.key_side[head] = key_columns(keys, r.neg[...], head).astype(LOW)
    plane.received(r.do_land, r.do_sems[layer])
    grads = r.do_land[...].reshape(SEQ_ALL, PAIR).astype(FULL)
    lane = lax.broadcasted_iota(jnp.int32, grads.shape, 1)
    r.do_side[0] = jnp.where(lane < HD, grads, 0.0).astype(LOW)
    r.do_side[1] = jnp.where(lane >= HD, grads, 0.0).astype(LOW)
    grads_t = r.do_land[...].reshape(SEQ_ALL, PAIR).T.astype(FULL)
    inner = []
    for head in range(2):
        side = slice(head * HD, (head + 1) * HD)
        inner.append(
            jnp.concatenate(
                [
                    jnp.sum(turned[at, side] * grads_t[side, at * BS : (at + 1) * BS], axis=0, keepdims=True)
                    for at in range(SEQ_ALL // BS)
                ],
                axis=1,
            )
        )
    left = lax.broadcasted_iota(jnp.int32, (BS, PAIR), 1) < HD
    keys_held = [keys_t[head * HD : (head + 1) * HD] for head in range(2)]
    for at in range(SEQ_ALL // BS):
        first = at * BS
        grad_k = []
        grad_v = None
        values = held[2, 2 * at : 2 * at + 2].reshape(BS, PAIR)
        for head in range(2):
            scores = dot_t(r.key_side[head, first : first + BS], r.query_side[head])
            probs = jnp.exp(scores - stats[head : head + 1])
            dprobs = dot_t(values, r.do_side[head])
            dscores = (probs * (dprobs - inner[head])).astype(LOW)
            term = dot(probs.astype(LOW), r.do_side[head])
            grad_v = term if grad_v is None else grad_v + term
            grad_k.append(dot(dscores, r.query_plain[head]))
            r.grad_q[head * HD : (head + 1) * HD] += dot(keys_held[head][:, first : first + BS], dscores)
        grad_k = jnp.where(left, grad_k[0], grad_k[1]).astype(LOW)
        grad_v = grad_v.astype(LOW)
        for half in range(2):
            to = 2 * at + half
            rows = slice(half * TOKENS, (half + 1) * TOKENS)
            r.dkv_message[to, :, :PAIR] = grad_k[rows]
            r.dkv_message[to, :, PAIR:] = grad_v[rows]
            plane.send_or_keep(r.dkv_message, r.dkv_land, r.dkv_sems[layer], to)
    for j in range(8):
        r.dq_message[j] = (r.grad_q[:, j * TOKENS : (j + 1) * TOKENS] * HD**-0.5).astype(LOW).T
        plane.send_or_keep(r.dq_message, r.dq_land, r.dq_sems[layer], j)


class Refs:
    pass


def names(**given):
    return tuple(given)


SCRATCH = dict(
    weights=pltpu.VMEM((NB, BS, BS), LOW),
    wide=pltpu.VMEM((2, QUART, BS, BS), FULL),
    notes=pltpu.VMEM((8, TOKENS), FULL),
    notes_land=pltpu.VMEM((8, 8, TOKENS), FULL),
    rows_land=pltpu.VMEM((1, TOKENS, D), LOW),
    first_land=pltpu.VMEM((1, TOKENS, D), LOW),
    second_land=pltpu.VMEM((1, TOKENS, D), LOW),
    pred_one=pltpu.VMEM((1, TOKENS, D), LOW),
    pred_two=pltpu.VMEM((1, TOKENS, D), LOW),
    hidden_one=pltpu.VMEM((TOKENS, D), FULL),
    hidden_two=pltpu.VMEM((TOKENS, D), FULL),
    middle_one=pltpu.VMEM((TOKENS, D), FULL),
    slope_one=pltpu.VMEM((DEEP, TOKENS, BS), FULL),
    slope_two=pltpu.VMEM((DEEP, TOKENS, BS), FULL),
    act_held=pltpu.VMEM((TOKENS, FF), LOW),
    left_held=pltpu.VMEM((2, 3 * WIDE + DEEP, BS, TOKENS), LOW),
    right_held=pltpu.VMEM((2, 5 * WIDE + DEEP, TOKENS, BS), LOW),
    packed=pltpu.VMEM((3, 8, TOKENS, PAIR), LOW),
    held=pltpu.VMEM((2, 3, 8, TOKENS, PAIR), LOW),
    values_t=pltpu.VMEM((PAIR, SEQ_ALL), LOW),
    expos=pltpu.VMEM((2, SEQ_ALL, BS), LOW),
    turned=pltpu.VMEM((2, SEQ_ALL // BS, PAIR, BS), FULL),
    stats=pltpu.VMEM((2, 8, SEQ_ALL), FULL),
    o_message=pltpu.VMEM((8, TOKENS, PAIR), LOW),
    o_land=pltpu.VMEM((8, TOKENS, PAIR), LOW),
    do_message=pltpu.VMEM((8, TOKENS, PAIR), LOW),
    do_land=pltpu.VMEM((8, TOKENS, PAIR), LOW),
    dq_message=pltpu.VMEM((8, TOKENS, PAIR), LOW),
    dq_land=pltpu.VMEM((8, TOKENS, PAIR), LOW),
    dkv_message=pltpu.VMEM((8, TOKENS, 2 * PAIR), LOW),
    dkv_land=pltpu.VMEM((8, TOKENS, 2 * PAIR), LOW),
    neg=pltpu.VMEM((SEQ_ALL, PAIR), FULL),
    query_side=pltpu.VMEM((2, SEQ_ALL, PAIR), LOW),
    query_plain=pltpu.VMEM((2, SEQ_ALL, PAIR), LOW),
    key_side=pltpu.VMEM((2, SEQ_ALL, PAIR), LOW),
    do_side=pltpu.VMEM((2, SEQ_ALL, PAIR), LOW),
    grad_q=pltpu.VMEM((PAIR, SEQ_ALL), FULL),
    load_sems=pltpu.SemaphoreType.DMA((7,)),
    z_sems=pltpu.SemaphoreType.DMA((2, 5, 2, 4)),
    y_sems=pltpu.SemaphoreType.DMA((2, 4, 4)),
    x_sems=pltpu.SemaphoreType.DMA((2, 2, 8)),
    core_sems=pltpu.SemaphoreType.DMA((2, 4, 8)),
    far_sems=pltpu.SemaphoreType.DMA((2, 2, 8)),
    note_send=pltpu.SemaphoreType.DMA((8,)),
    note_recv=pltpu.SemaphoreType.DMA((8,)),
    swap_local=pltpu.SemaphoreType.DMA((5,)),
    swap_send=pltpu.SemaphoreType.DMA((5,)),
    swap_recv=pltpu.SemaphoreType.DMA((5,)),
    plane_sems=pltpu.SemaphoreType.DMA((2, 7, 2, 8)),
    pool_sems=pltpu.SemaphoreType.DMA((3, 16)),
)
INPUTS = names(slots=0, lead_steps=0, flags=0, masters=0, rows_in=0, first_in=0, second_in=0, vectors=0)
OUTPUTS = names(left_pool=0, right_pool=0, pred_one_out=0, pred_two_out=0, input_grad=0, rows=0)


def model_kernel(*refs):
    r = Refs()
    for name, ref in zip(INPUTS + OUTPUTS + tuple(SCRATCH), refs):
        setattr(r, name, ref)
    for name in ("held", "turned", "stats"):
        setattr(r, name, [getattr(r, name).at[layer] for layer in range(2)])
    r.in_sems = [r.plane_sems.at[layer, pl.ds(0, 3)] for layer in range(2)]
    for at, name in enumerate(("o_sems", "do_sems", "dq_sems", "dkv_sems")):
        setattr(r, name, [r.plane_sems.at[layer, 3 + at] for layer in range(2)])
    swaps = [Swap(r.swap_local, r.swap_send, r.swap_recv, at) for at in range(5)]
    r.swap_rows = swaps[0]
    r.plane = Plane()
    vecs = r.vectors
    weights = Weights(r.slots, r.weights)

    def while_last():
        swaps[0].finish()
        r.rows[...] = jnp.zeros_like(r.rows)
        for layer in range(2):
            r.stats[layer][...] = jnp.zeros((8, SEQ_ALL), FULL)

    lane = lax.broadcasted_iota(jnp.int32, (1, TOKENS), 1)
    r.notes[...] = jnp.zeros_like(r.notes)
    r.notes[0:1] = r.flags[...].astype(FULL) - 1.0
    for at in range(2):
        r.notes[1:2] += jnp.where(lane == at, r.lead_steps[at, 0].astype(FULL), 0.0)
    gather_blocks(r, r.notes, while_last)
    mask_columns(r.notes_land, r.neg)
    leads = [r.notes_land[0, 1:2, at : at + 1] for at in range(2)]
    r.hidden_one[...] = r.rows_land[0].astype(FULL) + lead_row(vecs, leads[0])
    project(r, 0, r.hidden_one[...], vecs, weights)
    attend(r, 0)
    swaps[1].start(r.second_in, r.second_land)
    middle, result = feed(r, 0, r.hidden_one[...], vecs, weights, r.slope_one)
    r.middle_one[...] = middle
    r.pred_one[0] = result.astype(LOW)
    r.hidden_two[...] = result + lead_row(vecs, leads[1])
    project(r, 1, r.hidden_two[...], vecs, weights)
    attend(r, 1)
    swaps[3].start(r.pred_one, r.pred_one_out)
    middle, result = feed(r, 1, r.hidden_two[...], vecs, weights, r.slope_two)
    r.pred_two[0] = result.astype(LOW)
    swaps[2].start(r.first_in, r.first_land)
    swaps[1].finish()
    grad_middle = feed_back(r, 1, r.second_land[0].astype(FULL), middle, r.slope_two, vecs, weights)
    attend_back(r, 1)
    grad = project_back(r, 1, grad_middle, r.hidden_two[...], vecs, weights, leads[1])
    for source, sems in ((r.do_message, r.do_sems), (r.dkv_message, r.dkv_sems), (r.dq_message, r.dq_sems)):
        r.plane.sent(source, sems[1])
    swaps[2].finish()
    swaps[4].start(r.pred_two, r.pred_two_out)
    grad = grad + r.first_land[0].astype(FULL)
    grad_middle = feed_back(r, 0, grad, r.middle_one[...], r.slope_one, vecs, weights)
    attend_back(r, 0)
    grad = project_back(r, 0, grad_middle, r.hidden_one[...], vecs, weights, leads[0])
    r.input_grad[0] = grad.astype(LOW)
    for source, sems in ((r.do_message, r.do_sems), (r.dkv_message, r.dkv_sems), (r.dq_message, r.dq_sems)):
        r.plane.sent(source, sems[0])
    for left in (True, False):
        for layer in range(2):
            for kind in range(4):
                for copy in pool_copies(r, left, layer, kind):
                    copy.wait()
    swaps[3].finish()
    swaps[4].finish()


def model(slots, lead_steps, flags, masters, rows, first, second, vectors):
    return pl.pallas_call(
        model_kernel,
        out_shape=(
            shape((N_LEFT, BS, 4 * TOKENS)),
            shape((N_RIGHT, 4 * TOKENS, BS)),
            SHAPES["pred"],
            SHAPES["pred"],
            SHAPES["pred"],
            SHAPES["rows"],
        ),
        in_specs=[SMEM_IN] * 2 + [VMEM_AT] + [ANY_AT] * 4 + [VMEM_AT],
        out_specs=(ANY_AT,) * 4 + (VMEM_AT,) * 2,
        scratch_shapes=list(SCRATCH.values()),
        compiler_params=pltpu.CompilerParams(
            collective_id=0, has_side_effects=True, vmem_limit_bytes=63 * 1024 * 1024
        ),
        cost_estimate=pl.CostEstimate(flops=24 << 30, bytes_accessed=60 << 20, transcendentals=1 << 23),
        name="model",
    )(slots, lead_steps, flags, masters, rows, first, second, vectors)


SMEM_IN = pl.BlockSpec(memory_space=pltpu.SMEM)
VMEM_AT = pl.BlockSpec(memory_space=pltpu.VMEM)
ANY_AT = pl.BlockSpec(memory_space=pl.ANY)


def shape(dims, kind=LOW):
    return jax.ShapeDtypeStruct(dims, kind)


SHAPES = {"pred": shape((1, TOKENS, D)), "rows": shape((20, D), FULL)}


def bias_pieces():
    left = masked
    pieces = []
    for unused in range(3):
        piece = float(ml_dtypes.bfloat16(left))
        pieces.append(piece)
        left -= piece
    assert left == 0.0
    return pieces


MASK_PIECES = bias_pieces()


def own_columns(like, head):
    lane = lax.broadcasted_iota(jnp.int32, like.shape, 1)
    return (lane < HD) if head == 0 else (lane >= HD), lane - (HD if head == 0 else 0)


def key_columns(keys, neg, head):
    own, spot = own_columns(keys, head)
    side = jnp.zeros_like(keys)
    for at, piece in enumerate(MASK_PIECES):
        side = jnp.where(spot == at, neg * piece, side)
    return jnp.where(own, keys, side)


def query_columns(queries, head):
    own, spot = own_columns(queries, head)
    return jnp.where(own, queries * HD**-0.5, jnp.where((spot >= 0) & (spot < 3), 1.0, 0.0))


class Plane:
    def __init__(self):
        x, c, z, y = place()
        self.z = z
        self.me = 4 * c + 2 * x + y

    def device(self, j):
        return (turned_pair(lax.div(j, 2)), 2 * self.z + lax.rem(j, 2))

    def other(self, step):
        return lax.rem(self.me + step, 8)

    def others(self):
        return [self.device(self.other(step)) for step in range(1, 8)]

    def copy(self, src, dst, sems, send_at, recv_at, to):
        return pltpu.make_async_remote_copy(
            src_ref=src, dst_ref=dst, send_sem=sems.at[0, send_at], recv_sem=sems.at[1, recv_at],
            device_id=self.device(to), device_id_type=MESH,
        )

    def send(self, source, target, sems, to):
        self.copy(source.at[to], target.at[self.me], sems, to, self.me, to).start()

    def send_or_keep(self, source, target, sems, to):
        @pl.when(to != self.me)
        def away():
            self.send(source, target, sems, to)

        @pl.when(to == self.me)
        def keep():
            target[to] = source[to]

    def received(self, target, sems):
        for step in range(1, 8):
            j = self.other(step)
            self.copy(target.at[j], target.at[j], sems, j, j, j).wait_recv()

    def received_from(self, target, sems, j):
        @pl.when(j != self.me)
        def arrived():
            self.copy(target.at[j], target.at[j], sems, j, j, j).wait_recv()

    def sent(self, source, sems):
        for step in range(1, 8):
            j = self.other(step)
            self.copy(source.at[j], source.at[j], sems, j, j, j).wait_send()


def mask_columns(notes, neg):
    for j in range(8):
        neg[j * TOKENS : (j + 1) * TOKENS] = jnp.broadcast_to(notes[j, 0:1], (TOKENS, TOKENS)).T


LEFTS = (WIDE, WIDE, WIDE, DEEP)
RIGHTS = (3 * WIDE, WIDE, DEEP, WIDE)
LEFT_AT = (0, WIDE, 2 * WIDE, 3 * WIDE)
RIGHT_AT = (0, 3 * WIDE, 4 * WIDE, 4 * WIDE + DEEP)
N_LEFT = 3 * WIDE + DEEP
N_RIGHT = 5 * WIDE + DEEP


def pools_of(block):
    left = jnp.zeros_like(block)
    right = jnp.zeros_like(block)
    for at, base in enumerate((QKV_AT, OUT_AT, UP_AT, DOWN_AT)):
        inside = block >= base
        cols = RIGHTS[at]
        left = jnp.where(inside, LEFT_AT[at] + (block - base) // cols, left)
        right = jnp.where(inside, RIGHT_AT[at] + (block - base) % cols, right)
    return left, right


def halves(value):
    high = value.astype(LOW)
    return high, (value - high.astype(FULL)).astype(LOW)


def fine(left, right):
    return dot(
        jnp.concatenate([left[0], left[1], left[0]], axis=1),
        jnp.concatenate([right[0], right[0], right[1]], axis=0),
    )


def statistic(gram, shrink, diag, eye):
    return jnp.where(eye, 0.5 * diag, 0.0) + shrink * gram


def roots(stats, eye):
    scales = [jnp.sqrt(jnp.sum(jnp.sum(stat * stat, axis=1, keepdims=True), axis=0, keepdims=True)) for stat in stats]
    moving = [stat / scale for stat, scale in zip(stats, scales)]
    approx = [None] * len(stats)
    ahead = range(len(stats))
    for iteration in range(ITERS):
        factors = [(jnp.where(eye, 5.0, 0.0) - moving[i]) * 0.25 for i in ahead]
        parts = [halves(factor) for factor in factors]
        if iteration == 0:
            approx = [factors[i] * lax.rsqrt(jnp.sqrt(scales[i])) for i in ahead]
        else:
            approx = [fine(halves(approx[i]), parts[i]) for i in ahead]
        if iteration < ITERS - 1:
            squares = [halves(fine(parts[i], parts[i])) for i in ahead]
            fourths = [halves(fine(squares[i], squares[i])) for i in ahead]
            moving = [fine(fourths[i], halves(moving[i])) for i in ahead]
    return approx


PAIRED = 2
SUM_SCRATCH = dict(
    left_t=pltpu.VMEM((N_LEFT, BS, 4 * TOKENS), LOW),
    right_pool=pltpu.VMEM((N_RIGHT, 4 * TOKENS, BS), LOW),
    x_stage=pltpu.VMEM((2, 2, 4, PAIRED, BS, BS), LOW),
    x_land=pltpu.VMEM((2, 2, 4, PAIRED, BS, BS), LOW),
    yb_stage=pltpu.VMEM((4, QUART, BS, BS), LOW),
    yb_land=pltpu.VMEM((4, QUART, BS, BS), LOW),
    ym_stage=pltpu.VMEM((2, 4, PAIRED, BS, BS), LOW),
    ym_land=pltpu.VMEM((2, 4, PAIRED, BS, BS), LOW),
    zb_stage=pltpu.VMEM((4, QUART, BS, BS), LOW),
    zb_land=pltpu.VMEM((3, QUART, BS, BS), LOW),
    zm_stage=pltpu.VMEM((2, 4, PAIRED, BS, BS), LOW),
    zm_land=pltpu.VMEM((2, 3, PAIRED, BS, BS), LOW),
    both_stage=pltpu.VMEM((2, PAIRED, BS, BS), LOW),
    both_land=pltpu.VMEM((PAIRED, BS, BS), LOW),
    own=pltpu.VMEM((6, BS, BS), LOW),
    staged=pltpu.VMEM((6, BS, BS), LOW),
    pair_rows=pltpu.VMEM((20, D), FULL),
    chip_rows=pltpu.VMEM((20, D), FULL),
    plane_rows=pltpu.VMEM((20, D), FULL),
    row_land=pltpu.VMEM((3, 20, D), FULL),
    row_z=pltpu.VMEM((4, 20, D), FULL),
    pool_sems=pltpu.SemaphoreType.DMA((2,)),
    send_sems=pltpu.SemaphoreType.DMA((11, 4)),
    recv_sems=pltpu.SemaphoreType.DMA((11, 4)),
    row_send=pltpu.SemaphoreType.DMA((6,)),
    row_recv=pltpu.SemaphoreType.DMA((6,)),
    share_send=pltpu.SemaphoreType.DMA((6, 6)),
    share_recv=pltpu.SemaphoreType.DMA((6, 6)),
    local_sems=pltpu.SemaphoreType.DMA((9,)),
    swap_local=pltpu.SemaphoreType.DMA((1,)),
    swap_send=pltpu.SemaphoreType.DMA((1,)),
    swap_recv=pltpu.SemaphoreType.DMA((1,)),
)
SUM_INPUTS = names(left_ids=0, right_ids=0, rows_in=0, left_diag=0, right_diag=0, grad_in=0, left_in=0, right_in=0)
SUM_OUTPUTS = names(rows_out=0, grads_out=0, moves_out=0, grad_out=0)


def update_kernel(*refs):
    r = Refs()
    for name, ref in zip(SUM_INPUTS + SUM_OUTPUTS + tuple(SUM_SCRATCH), refs):
        setattr(r, name, ref)
    here = [
        pltpu.make_async_copy(r.right_in, r.right_pool, r.pool_sems.at[0]),
        pltpu.make_async_copy(r.left_in, r.left_t, r.pool_sems.at[1]),
    ]
    for copy in here:
        copy.start()
    x, c, z, y = place()
    samp = 2 * x + c
    blk = 2 * z + y
    to_c = (2 * x + 1 - c, blk)
    to_x = (2 * (1 - x) + c, blk)
    to_y = (samp, 2 * z + 1 - y)
    to_z = [(samp, 2 * lax.rem(z + step, 4) + y) for step in (1, 2, 3)]
    meet_all()
    swap = Swap(r.swap_local, r.swap_send, r.swap_recv)
    swap.start(r.grad_in, r.grad_out)
    row_copies = [push(r.rows_in, r.row_land.at[0], r.row_send.at[0], r.row_recv.at[0], to_c)]
    eye = lax.broadcasted_iota(jnp.int32, (BS, BS), 0) == lax.broadcasted_iota(jnp.int32, (BS, BS), 1)

    def group(half, k):
        return 2 * lax.rem(z + 1 + k, 4) + (1 - y if half == 0 else y)

    def part(half, k, offset, count=PAIRED):
        slot = group(half, k) * GROUP + c * HALF + offset
        return [dot(r.left_t[r.left_ids[slot + i]], r.right_pool[r.right_ids[slot + i]]) for i in range(count)]

    def mine(batch):
        return x * 8 + PAIRED * batch

    def other(batch):
        return (1 - x) * 8 + PAIRED * batch

    both = QUART

    def link(kind, k, stage, land, to):
        return pltpu.make_async_remote_copy(
            src_ref=stage, dst_ref=land, send_sem=r.send_sems.at[kind, k], recv_sem=r.recv_sems.at[kind, k],
            device_id=to, device_id_type=MESH,
        )

    def along_x(batch, half, k):
        return link(2 * batch + half, k, r.x_stage.at[batch, half, k], r.x_land.at[batch, half, k], to_x)

    def along_y_both(k):
        return link(4, k, r.yb_stage.at[k], r.yb_land.at[k], to_y)

    def along_y(batch, k):
        return link(5 + batch, k, r.ym_stage.at[batch, k], r.ym_land.at[batch, k], to_y)

    def along_z_both(k):
        return link(7, k, r.zb_stage.at[k], r.zb_land.at[k], (samp, group(1, k)))

    def along_z(batch, k):
        return link(8 + batch, k, r.zm_stage.at[batch, k], r.zm_land.at[batch, k], (samp, group(1, k)))

    def last():
        return link(10, 0, r.both_stage.at[1 - x], r.both_land, to_x)

    def send_x(batch, half, k):
        for i, value in enumerate(part(half, k, other(batch))):
            r.x_stage[batch, half, k, i] = value.astype(LOW)
        along_x(batch, half, k).start()

    def add_x_send_y(batch, k):
        values = part(0, k, mine(batch))
        along_x(batch, 0, k).wait_recv()
        for i, value in enumerate(values):
            r.ym_stage[batch, k, i] = (value + r.x_land[batch, 0, k, i].astype(FULL)).astype(LOW)
        along_y(batch, k).start()

    def add_both_send_z(batch, k):
        values = part(1, k, mine(batch))
        along_x(batch, 1, k).wait_recv()
        values = [value + r.x_land[batch, 1, k, i].astype(FULL) for i, value in enumerate(values)]
        along_y(batch, k).wait_recv()
        for i, value in enumerate(values):
            r.zm_stage[batch, k, i] = (value + r.ym_land[batch, k, i].astype(FULL)).astype(LOW)

        @pl.when(k < 3)
        def send_on():
            along_z(batch, k).start()

    def each(step):
        def body(k, carry):
            step(k)
            return carry

        lax.fori_loop(0, 4, body, 0)

    def slot_of(i, far=False):
        side = (1 - x) if far else x
        return c * HALF + (side * 8 + i if i < QUART else QUART + 2 * side + i - QUART)

    def share(kind, k, src, dst, to):
        return pltpu.make_async_remote_copy(
            src_ref=src, dst_ref=dst, send_sem=r.share_send.at[kind, k], recv_sem=r.share_recv.at[kind, k],
            device_id=to, device_id_type=MESH,
        )

    def grad_to(kind, pair, to):
        place_out = r.grads_out.at[pl.ds(slot_of(PAIRED * pair), PAIRED)]
        return share(kind, pair, r.own.at[pl.ds(PAIRED * pair, PAIRED)], place_out, to)

    def grad_on(pair):
        place_out = r.grads_out.at[pl.ds(slot_of(PAIRED * pair, True), PAIRED)]
        return share(2, pair, place_out, place_out, to_c)

    def grad_kept(pair):
        place_out = r.grads_out.at[pl.ds(slot_of(PAIRED * pair), PAIRED)]
        return pltpu.make_async_copy(r.own.at[pl.ds(PAIRED * pair, PAIRED)], place_out, r.local_sems.at[6 + pair])

    def move_to(kind, i, to):
        return share(kind, i, r.staged.at[i], r.moves_out.at[slot_of(i)], to)

    def move_on(i):
        place_out = r.moves_out.at[slot_of(i, True)]
        return share(5, i, place_out, place_out, to_c)

    def move_kept(i):
        return pltpu.make_async_copy(r.staged.at[i], r.moves_out.at[slot_of(i)], r.local_sems.at[i])

    def share_grads(pair):
        grad_to(0, pair, to_x).start()
        grad_to(1, pair, to_c).start()
        grad_kept(pair).start()

    def directions(pair):
        held = []
        stats = []
        for i in range(PAIRED * pair, PAIRED * pair + PAIRED):
            low = r.own[i]
            grad = low.astype(FULL)
            mean = jnp.sum(jnp.sum(grad * grad, axis=1, keepdims=True), axis=0, keepdims=True) / (BS * BS)
            shrink = 0.5 / (mean + 1e-06)
            low_t = grad.T.astype(LOW)
            slot = slot_of(i)
            stats.append(statistic(dot(low, low_t), shrink, r.left_diag[pl.ds(slot, 1)], eye))
            stats.append(statistic(dot(low_t, low), shrink, r.right_diag[pl.ds(slot, 1)], eye))
            held.append((i, low, lax.rsqrt(mean + 1e-06)))
        sides = roots(stats, eye)
        for n, (i, low, rate) in enumerate(held):
            high, rest = halves(sides[2 * n])
            turned = dot(jnp.concatenate([high, rest], axis=1), jnp.concatenate([low, low], axis=0)) * rate
            r.staged[i] = fine(halves(turned), halves(sides[2 * n + 1])).astype(LOW)
            move_to(3, i, to_x).start()
            move_to(4, i, to_c).start()
            move_kept(i).start()

    def finish_batch(batch):
        for k in range(3):
            along_z(batch, k).wait_recv()
        for i in range(PAIRED):
            value = r.zm_stage[batch, 3, i].astype(FULL)
            for k in range(3):
                value = value + r.zm_land[batch, k, i].astype(FULL)
            r.own[PAIRED * batch + i] = value.astype(LOW)
        share_grads(batch)

    def pass_on(pair):
        grad_to(0, pair, to_x).wait_recv()
        grad_on(pair).start()
        for i in range(PAIRED * pair, PAIRED * pair + PAIRED):
            move_to(3, i, to_x).wait_recv()
            move_on(i).start()

    for copy in here:
        copy.wait()

    @each
    def begin(k):
        for i, value in enumerate(part(0, k, both, QUART)):
            r.yb_stage[k, i] = value.astype(LOW)
        along_y_both(k).start()
        send_x(0, 0, k)

    @each
    def more(k):
        send_x(0, 1, k)

    row_copies[0].wait_recv()
    r.pair_rows[...] = r.rows_in[...] + r.row_land[0]
    row_copies.append(push(r.pair_rows, r.row_land.at[1], r.row_send.at[1], r.row_recv.at[1], to_x))

    @each
    def middle(k):
        add_x_send_y(0, k)
        values = part(1, k, both, QUART)
        along_y_both(k).wait_recv()
        for i, value in enumerate(values):
            r.zb_stage[k, i] = (value + r.yb_land[k, i].astype(FULL)).astype(LOW)

        @pl.when(k < 3)
        def send_on():
            along_z_both(k).start()

        send_x(1, 0, k)

    row_copies[1].wait_recv()
    r.chip_rows[...] = r.pair_rows[...] + r.row_land[1]
    row_copies.append(push(r.chip_rows, r.row_land.at[2], r.row_send.at[2], r.row_recv.at[2], to_y))

    @each
    def late(k):
        add_both_send_z(0, k)

    for k in range(3):
        along_z_both(k).wait_recv()
    for i in range(QUART):
        value = r.zb_stage[3, i].astype(FULL)
        for k in range(3):
            value = value + r.zb_land[k, i].astype(FULL)
        r.both_stage[i // 2, i % 2] = value.astype(LOW)
    last().start()

    @each
    def more_again(k):
        send_x(1, 1, k)

    @each
    def middle_again(k):
        add_x_send_y(1, k)

    row_copies[2].wait_recv()
    r.plane_rows[...] = r.chip_rows[...] + r.row_land[2]
    for step in range(3):
        row_copies.append(
            push(r.plane_rows, r.row_z.at[z], r.row_send.at[3 + step], r.row_recv.at[3 + step], to_z[step])
        )
    r.row_z[z] = r.plane_rows[...]
    last().wait_recv()
    for i in range(PAIRED):
        r.own[QUART + i] = (r.both_stage[x, i].astype(FULL) + r.both_land[i].astype(FULL)).astype(LOW)
    share_grads(2)
    directions(2)

    @each
    def late_again(k):
        add_both_send_z(1, k)

    finish_batch(0)
    directions(0)
    for step in range(3):
        row_copies[3 + step].wait_recv()
    r.rows_out[...] = (r.row_z[0] + r.row_z[1]) + (r.row_z[2] + r.row_z[3])
    finish_batch(1)
    pass_on(2)
    directions(1)
    pass_on(0)
    pass_on(1)
    for pair in range(3):
        grad_to(1, pair, to_c).wait_recv()
        grad_on(pair).wait_recv()
        grad_to(0, pair, to_x).wait_send()
        grad_to(1, pair, to_c).wait_send()
        grad_on(pair).wait_send()
        grad_kept(pair).wait()
    for i in range(6):
        move_to(4, i, to_c).wait_recv()
        move_on(i).wait_recv()
        move_to(3, i, to_x).wait_send()
        move_to(4, i, to_c).wait_send()
        move_on(i).wait_send()
        move_kept(i).wait()
    for copy in row_copies:
        copy.wait_send()
    last().wait_send()

    @each
    def drain(k):
        along_y_both(k).wait_send()
        for batch in range(2):
            along_x(batch, 0, k).wait_send()
            along_x(batch, 1, k).wait_send()
            along_y(batch, k).wait_send()

        @pl.when(k < 3)
        def sent_on():
            along_z_both(k).wait_send()
            for batch in range(2):
                along_z(batch, k).wait_send()

    swap.finish()


def update(left_ids, right_ids, rows, left_start, right_start, grad, left_pool, right_pool):
    return pl.pallas_call(
        update_kernel,
        out_shape=(SHAPES["rows"], shape((GROUP, BS, BS)), shape((GROUP, BS, BS)), SHAPES["pred"]),
        in_specs=[SMEM_IN] * 2 + [VMEM_AT] * 3 + [ANY_AT] * 3,
        out_specs=(VMEM_AT,) + (ANY_AT,) * 3,
        scratch_shapes=list(SUM_SCRATCH.values()),
        compiler_params=pltpu.CompilerParams(
            collective_id=1, has_side_effects=True, vmem_limit_bytes=VMEM_ASK
        ),
        cost_estimate=pl.CostEstimate(flops=36 << 30, bytes_accessed=40 << 20, transcendentals=0),
        name="update",
    )(left_ids, right_ids, rows, left_start, right_start, grad, left_pool, right_pool)


STEP = 8


def finish_kernel(
    grad, move, weight, left_diag, right_diag, rows, vecs, moment, input_grad, pred_one, pred_two,
    grad_out, left_out, right_out, new_out, low_out,
    rows_out, moment_out, vecs_out, input_out, pred_one_out, pred_two_out,
):
    eye = lax.broadcasted_iota(jnp.int32, (BS, BS), 0) == lax.broadcasted_iota(jnp.int32, (BS, BS), 1)
    at = pl.program_id(0)

    def mean(value):
        return jnp.sum(jnp.sum(value, axis=1, keepdims=True), axis=0, keepdims=True) / (BS * BS)

    for i in range(STEP):
        low = grad[i]
        full = low.astype(FULL)
        grad_out[i] = full
        shrink = 0.5 / (mean(full * full) + 1e-06)
        low_t = full.T.astype(LOW)
        left_out[i] = statistic(dot(low, low_t), shrink, left_diag[pl.ds(at * STEP + i, 1)], eye)
        right_out[i] = statistic(dot(low_t, low), shrink, right_diag[pl.ds(at * STEP + i, 1)], eye)
        step = move[i].astype(FULL)
        start = weight[i]
        ratio = jnp.sqrt(mean(start * start)) * lax.rsqrt(mean(step * step) + 1e-06)
        new = start - step_rate * ratio * step
        new_out[i] = new
        low_out[i] = new.astype(LOW)

    @pl.when(at == 0)
    def small():
        value = rows[...]
        scaled = value * lax.rsqrt(jnp.mean(value * value, axis=1, keepdims=True) + 1e-06)
        moments = 0.5 * moment[...] + 0.5 * scaled * scaled
        rows_out[...] = value
        moment_out[...] = moments
        vecs_out[...] = vecs[...] - vector_rate * scaled * lax.rsqrt(moments)
        input_out[...] = input_grad[...].astype(FULL)
        pred_one_out[...] = pred_one[...]
        pred_two_out[...] = pred_two[...]


def finish_slots(grads, moves, masters, left_start, right_start, rows, vecs, moment, input_grad, pred_one, pred_two):
    block = pl.BlockSpec((STEP, BS, BS), lambda i: (i, 0, 0))
    diag = pl.BlockSpec((GROUP, BS), lambda i: (0, 0))
    row = pl.BlockSpec((20, D), lambda i: (0, 0))
    wide = pl.BlockSpec((1, TOKENS, D), lambda i: (0, 0, 0))
    return pl.pallas_call(
        finish_kernel,
        grid=(GROUP // STEP,),
        compiler_params=pltpu.CompilerParams(vmem_limit_bytes=VMEM_ASK),
        out_shape=tuple(shape((GROUP, BS, BS), kind) for kind in (FULL, FULL, FULL, FULL, LOW))
        + (SHAPES["rows"],) * 3
        + (shape((1, TOKENS, D), FULL),)
        + (SHAPES["pred"],) * 2,
        in_specs=[block, block, block, diag, diag, row, row, row, wide, wide, wide],
        out_specs=(block,) * 5 + (row,) * 3 + (wide,) * 3,
        cost_estimate=pl.CostEstimate(flops=2 << 30, bytes_accessed=41 << 20, transcendentals=0),
        name="finish_slots",
    )(grads, moves, masters, left_start, right_start, rows, vecs, moment, input_grad, pred_one, pred_two)


def local_tuned(
    inputs,
    cot_first,
    cot_second,
    valid_flags,
    lead_steps,
    masters,
    assignment,
    left_start,
    right_start,
    vectors,
    vec_moment,
):
    left_pool, right_pool, pred_one, pred_two, input_grad, rows = model(
        assignment, lead_steps, valid_flags, masters, inputs, cot_first, cot_second, vectors
    )
    position = jnp.arange(NB, dtype=jnp.int32)
    inverse = jnp.sum(
        jnp.where(assignment[None, :] == position[:, None], position[None, :], 0), axis=1
    )
    left_ids, right_ids = pools_of(inverse)
    vec_grads, grads, moves, input_grad = update(
        left_ids, right_ids, rows, left_start, right_start, input_grad, left_pool, right_pool
    )
    (
        matrix_grads, left_stats, right_stats, new_masters, new_copies,
        vec_grads, vec_moments, new_vectors, input_grad, pred_one, pred_two,
    ) = finish_slots(
        grads, moves, masters, left_start, right_start, vec_grads, vectors, vec_moment, input_grad, pred_one, pred_two
    )
    return (
        pred_one,
        pred_two,
        input_grad,
        matrix_grads,
        left_stats,
        right_stats,
        new_masters,
        new_copies,
        vec_grads,
        vec_moments,
        new_vectors,
    )


def solution(mesh):
    placed = (
        P("samp", "blk", None),
        P("samp", "blk", None),
        P("samp", "blk", None),
        P("samp", "blk"),
        P(None, "samp"),
        P("blk", None, None),
        P(),
        P("blk", None),
        P("blk", None),
        P(),
        P(),
    )
    fits = mesh.shape["samp"] == 4 and mesh.shape["blk"] == 8
    return jax.shard_map(
        local_tuned if fits else local_any,
        mesh=mesh,
        in_specs=placed,
        out_specs=(
            P("samp", "blk", None),
            P("samp", "blk", None),
            P("samp", "blk", None),
            P("blk", None, None),
            P("blk", None, None),
            P("blk", None, None),
            P("blk", None, None),
            P("blk", None, None),
            P(),
            P(),
            P(),
        ),
        check_vma=False,
    )
```

profile of v0, /device:TPU:3, one launch (start us, length us, event | category | flops | bytes accessed | tf_op | source)
XLA Modules:
  0.0 392.0 jit_solution(5711591366309961019)
XLA Ops:
  0.6 1.3 copy.23.refs_1_
  1.9 0.8 select_reduce_fusion
  2.7 0.6 fusion.1
  3.3 223.9 %model.1 = (bf16[28,256,512]{2,1,0:T(8,128)(2,1)}, bf16[36,512,256]{2,1,0:T(8,128)(2,1)}, bf16[1,128,1024]{2,1,0:T(8,128)(2,1)}, bf16[1,128,1024]{2,1,0:T(8,128)...) custom-call(s32[192]{0:T(256)} %refs_0_.1, s32[2,1]{1,0:T(2,128)} %copy.23.refs_1_, s32[1,128]{1,0:T(1,128)} %refs_2_.1, ...), custom_call_target="tpu_custom_call" | custom-call | flops 25769803776 | bytes 62914560 | tf_op jit(solution)/shard_map/model/pallas_call | solution.py:1294
  227.3 148.4 %update.1 = (f32[20,1024]{1,0:T(8,128)}, bf16[24,256,256]{2,1,0:T(8,128)(2,1)}, bf16[24,256,256]{2,1,0:T(8,128)(2,1)}, bf16[1,128,1024]{2,1,0:T(8,128)(2,1)}) custom-call(s32[192]{0:T(256)} %get-tuple-element.54.refs_0_, s32[192]{0:T(256)} %get-tuple-element.53.refs_1_, f32[20,1024]{1,0:T(8,128)} %get-tuple-element.32.refs_2_, f32[24,256]{1,0:T(8,128)} %left_diag.1, ...), custom_call_target="tpu_custom_call" | custom-call | flops 38654705664 | bytes 41943040 | tf_op jit(solution)/shard_map/update/pallas_call | solution.py:1795
  375.7 16.0 %finish_slots.1 = (f32[24,256,256]{2,1,0:T(8,128)}, f32[24,256,256]{2,1,0:T(8,128)}, f32[24,256,256]{2,1,0:T(8,128)}, f32[24,256,256]{2,1,0:T(8,128)}, bf16[24,2...) custom-call(bf16[24,256,256]{2,1,0:T(8,128)(2,1)} %get-tuple-element, ...), custom_call_target="tpu_custom_call" | custom-call | flops 2147483648 | bytes 42991616 | tf_op jit(solution)/shard_map/finish_slots/pallas_call | solution.py:1856
where the time goes:
time: 394 us; the launch traced here: 392 us
  Pallas kernels  388 us (98%)
    pallas_call x1, Pallas kernels, model(): pl.pallas_call(model_kernel, out_shape=(shape((N_LEFT, BS, 4 * TOKENS)),...  224 us
    pallas_call x1, Pallas kernels, update(): pl.pallas_call(update_kernel, out_shape=(SHAPES['rows'], shape((GROUP, BS...  148 us
    pallas_call x1, Pallas kernels, finish_slots(): pl.pallas_call(finish_kernel, grid=(GROUP // STEP,), compiler_params=pltp...  16 us

commit v1 on v0

--- a/solution.py
+++ b/solution.py
@@ -1628,12 +1628,13 @@
     def move_kept(i):
         return pltpu.make_async_copy(r.staged.at[i], r.moves_out.at[slot_of(i)], r.local_sems.at[i])
 
-    def share_grads(pair):
-        grad_to(0, pair, to_x).start()
+    def share_grads(pair, across=True):
+        if across:
+            grad_to(0, pair, to_x).start()
         grad_to(1, pair, to_c).start()
         grad_kept(pair).start()
 
-    def directions(pair):
+    def directions(pair, across=True):
         held = []
         stats = []
         for i in range(PAIRED * pair, PAIRED * pair + PAIRED):
@@ -1651,7 +1652,8 @@
             high, rest = halves(sides[2 * n])
             turned = dot(jnp.concatenate([high, rest], axis=1), jnp.concatenate([low, low], axis=0)) * rate
             r.staged[i] = fine(halves(turned), halves(sides[2 * n + 1])).astype(LOW)
-            move_to(3, i, to_x).start()
+            if across:
+                move_to(3, i, to_x).start()
             move_to(4, i, to_c).start()
             move_kept(i).start()
 
@@ -1739,13 +1741,16 @@
     last().wait_recv()
     for i in range(PAIRED):
         r.own[QUART + i] = (r.both_stage[x, i].astype(FULL) + r.both_land[i].astype(FULL)).astype(LOW)
-    share_grads(2)
-    directions(2)
+    share_grads(2, False)
+    directions(2, False)
 
     @each
     def late_again(k):
         add_both_send_z(1, k)
 
+    grad_to(0, 2, to_x).start()
+    for i in (QUART, QUART + 1):
+        move_to(3, i, to_x).start()
     finish_batch(0)
     directions(0)
     for step in range(3):

time: 394 us -> 398 us (1.010); the launches traced: 392 us -> 392 us
  no operation moved by 1% of the time
where the time goes in v1:
time: 398 us; the launch traced here: 392 us
  Pallas kernels  388 us (97%)
    pallas_call x1, Pallas kernels, model(): pl.pallas_call(model_kernel, out_shape=(shape((N_LEFT, BS, 4 * TOKENS)),...  224 us
    pallas_call x1, Pallas kernels, update(): pl.pallas_call(update_kernel, out_shape=(SHAPES['rows'], shape((GROUP, BS...  148 us
    pallas_call x1, Pallas kernels, finish_slots(): pl.pallas_call(finish_kernel, grid=(GROUP // STEP,), compiler_params=pltp...  16 us

profile of v1, /device:TPU:3, one launch (start us, length us, event | category | flops | bytes accessed | tf_op | source)
XLA Modules:
  0.0 392.0 jit_solution(9633182257224213034)
XLA Ops:
  0.6 1.3 copy.23.refs_1_
  1.9 0.8 select_reduce_fusion
  2.7 0.6 fusion.1
  3.3 223.9 %model.1 = (bf16[28,256,512]{2,1,0:T(8,128)(2,1)}, bf16[36,512,256]{2,1,0:T(8,128)(2,1)}, bf16[1,128,1024]{2,1,0:T(8,128)(2,1)}, bf16[1,128,1024]{2,1,0:T(8,128)...) custom-call(s32[192]{0:T(256)} %refs_0_.1, s32[2,1]{1,0:T(2,128)} %copy.23.refs_1_, s32[1,128]{1,0:T(1,128)} %refs_2_.1, ...), custom_call_target="tpu_custom_call" | custom-call | flops 25769803776 | bytes 62914560 | tf_op jit(solution)/shard_map/model/pallas_call | solution.py:1294
  227.3 148.4 %update.1 = (f32[20,1024]{1,0:T(8,128)}, bf16[24,256,256]{2,1,0:T(8,128)(2,1)}, bf16[24,256,256]{2,1,0:T(8,128)(2,1)}, bf16[1,128,1024]{2,1,0:T(8,128)(2,1)}) custom-call(s32[192]{0:T(256)} %get-tuple-element.54.refs_0_, s32[192]{0:T(256)} %get-tuple-element.53.refs_1_, f32[20,1024]{1,0:T(8,128)} %get-tuple-element.32.refs_2_, f32[24,256]{1,0:T(8,128)} %left_diag.1, ...), custom_call_target="tpu_custom_call" | custom-call | flops 38654705664 | bytes 41943040 | tf_op jit(solution)/shard_map/update/pallas_call | solution.py:1800
  375.7 16.0 %finish_slots.1 = (f32[24,256,256]{2,1,0:T(8,128)}, f32[24,256,256]{2,1,0:T(8,128)}, f32[24,256,256]{2,1,0:T(8,128)}, f32[24,256,256]{2,1,0:T(8,128)}, bf16[24,2...) custom-call(bf16[24,256,256]{2,1,0:T(8,128)(2,1)} %get-tuple-element, ...), custom_call_target="tpu_custom_call" | custom-call | flops 2147483648 | bytes 42991616 | tf_op jit(solution)/shard_map/finish_slots/pallas_call | solution.py:1861
